TPU v7x, 32 devices: a whole 2x2x4 slice. The times are simulated.
32 devices in a mesh: sub: 16 (over z, y, core), grp: 2 (over x).
Axes of the slice: x: 2, y: 2, z: 4, core: 2. Of those that a mesh axis runs over, the one named last changes fastest.
Arguments:
- margin_basis: bfloat16 [32, 6, 384, 128], P(('sub', 'grp')), may hold values from -6 to 6
- pair_matrix: bfloat16 [32, 6, 384, 384], P(('sub', 'grp')), as said below
- own_basis: bfloat16 [32, 2048, 128], P(('sub', 'grp')), may hold values from -0.125 to 0.125
- own_image: bfloat16 [32, 2048, 128], P(('sub', 'grp')), may hold values from -6 to 6
- tile_counts: int32 [32, 6], P(('sub', 'grp')), may hold values from 0 to 3, as said below
Outputs:
- coarse_rows: float32 [32, 7, 128, 128], P('sub', None, 'grp')
Inputs may be any that keep to these rules, and one draw needn't show every extreme that they name: `tile_counts`: tile counts of the two slots of one neighbour pair are equal, zero for slots without neighbour, and the pairs of subdomains 0 and 1 and of subdomains (7) * 2 and (8) * 2 have 3 tiles in every draw. pair_matrix[s + stride, 2j + 1] is the transpose of pair_matrix[s, 2j] wherever both are neighbours.
All inputs are finite; a program needn't handle non-finite values.
Results may differ from a plain program's by a relative error of at most 0.0026.
Values may be sent and summed in bfloat16 or wider, within the bound.
A program may use at most 64 MiB of HBM per device.

v0:
```python
import jax
import jax.numpy as jnp
from jax import lax
from jax.sharding import PartitionSpec as P

ROW_TILE = 128
SPAN = 8


def shifted(value, axis, steps):
    count = lax.axis_size(axis)
    initial, last = (max(0, -steps), min(count, count - steps))
    return lax.ppermute(value, axis, [(source, source + steps) for source in range(initial, last)])


def masked(block, tile_count):
    row_index = lax.broadcasted_iota(jnp.int32, block.shape, 0)
    return jnp.where(row_index < tile_count * ROW_TILE, block, jnp.zeros((), block.dtype))


def contract_rows(left, right):
    return lax.dot_general(
        left, right, (((0,), (0,)), ((), ())), preferred_element_type=jnp.float32
    )


def apply_block(matrix, column_basis, flipped):
    if flipped:
        return contract_rows(matrix, column_basis)
    return jnp.dot(matrix, column_basis, preferred_element_type=jnp.float32)


def couple_pair(matrix, row_basis, column_basis, flipped):
    applied = apply_block(matrix, column_basis, flipped).astype(jnp.bfloat16)
    return contract_rows(row_basis, applied)


def local(margin_basis, pair_matrix, own_basis, own_image, tile_counts):
    own_margin = margin_basis[0]
    matrices = pair_matrix[0]
    counts = tile_counts[0]
    x_above = shifted(own_margin[1], "grp", -1)
    y_above = shifted(own_margin[3], "sub", -1)
    z_above = shifted(own_margin[5], "sub", -SPAN)
    diagonal_block = contract_rows(own_basis[0], own_image[0])
    received = (x_above, y_above, z_above)
    upper_blocks = []
    for which in range(3):
        upper = 2 * which
        upper_blocks.append(
            couple_pair(
                matrices[upper],
                masked(own_margin[upper], counts[upper]),
                masked(received[which], counts[upper]),
                False,
            )
        )
    x_below = shifted(own_margin[0], "grp", 1)
    y_below = shifted(own_margin[2], "sub", 1)
    z_below = shifted(own_margin[4], "sub", SPAN)
    from_below = (x_below, y_below, z_below)
    lower_blocks = []
    for which in range(3):
        lower = 2 * which + 1
        lower_blocks.append(
            couple_pair(
                matrices[lower],
                masked(from_below[which], counts[lower]),
                masked(own_margin[lower], counts[lower]),
                True,
            ).T
        )
    blocks = [diagonal_block]
    for which in range(3):
        blocks.append(upper_blocks[which])
        blocks.append(lower_blocks[which])
    coarse = jnp.stack(blocks, axis=0)[None]
    return lax.all_to_all(coarse, "grp", split_axis=2, concat_axis=0, tiled=True)


def solution(mesh):
    return jax.shard_map(
        local,
        mesh=mesh,
        in_specs=(
            P(("sub", "grp"), None, None, None),
            P(("sub", "grp"), None, None, None),
            P(("sub", "grp"), None, None),
            P(("sub", "grp"), None, None),
            P(("sub", "grp"), None),
        ),
        out_specs=P("sub", None, "grp", None),
        check_vma=False,
    )
```

profile of v0, /device:TPU:0, one launch (start us, length us, event | category | flops | bytes accessed | tf_op | source)
XLA Modules:
  0.0 48.5 jit_solution(1184075745215286338)
XLA Ops:
  0.0 0.0 copy-start
  0.0 0.0 copy-start.1
  0.0 1.3 %slice_bitcast_fusion = (bf16[384,128]{1,0:T(8,128)(2,1)S(1)}, bf16[384,128]{1,0:T(8,128)(2,1)S(1)}, bf16[384,128]{1,0:T(8,128)(2,1)S(1)}, bf16[384,128]{1,0:T(8...) fusion(bf16[1,6,384,128]{3,2,1,0:T(8,128)(2,1)} %param.5), kind=kLoop, calls=%fused_computation.47 | loop fusion | bytes 1179648 | tf_op jit(solution)/shard_map/squeeze | solution.py:53
  1.3 5.9 %collective-permute-start.5 = (bf16[384,128]{1,0:T(8,128)(2,1)S(1)}, bf16[384,128]{1,0:T(8,128)(2,1)S(1)}, u32[]{:S(2)}, u32[]{:S(2)}) collective-permute-start(bf16[384,128]{1,0:T(8,128)(2,1)S(1)} %get-tuple-element.5), channel_id=1, source_target_pairs={{0,16},{2,18},{4,20},{6,22},{8,24},{10,26},{12,28},{14,30},{1,17},... | collective-permute-start | bytes 294920 | tf_op jit(solution)/shard_map/ppermute | solution.py:13
  7.2 1.3 %collective-permute-start.2 = (bf16[384,128]{1,0:T(8,128)(2,1)S(1)}, bf16[384,128]{1,0:T(8,128)(2,1)S(1)}, u32[]{:S(2)}, u32[]{:S(2)}) collective-permute-start(bf16[384,128]{1,0:T(8,128)(2,1)S(1)} %get-tuple-element.6), channel_id=1, source_target_pairs={{2,0},{4,2},{6,4},{8,6},{10,8},{12,10},{14,12},{16,14},{18,16},{20... | collective-permute-start | bytes 294920 | tf_op jit(solution)/shard_map/ppermute | solution.py:13
  8.5 3.0 %collective-permute-start.3 = (bf16[384,128]{1,0:T(8,128)(2,1)S(1)}, bf16[384,128]{1,0:T(8,128)(2,1)S(1)}, u32[]{:S(2)}, u32[]{:S(2)}) collective-permute-start(bf16[384,128]{1,0:T(8,128)(2,1)S(1)} %get-tuple-element.7), channel_id=1, source_target_pairs={{0,2},{2,4},{4,6},{6,8},{8,10},{10,12},{12,14},{14,16},{16,18},{18... | collective-permute-start | bytes 294920 | tf_op jit(solution)/shard_map/ppermute | solution.py:13
  11.6 1.3 %collective-permute-start = (bf16[384,128]{1,0:T(8,128)(2,1)S(1)}, bf16[384,128]{1,0:T(8,128)(2,1)S(1)}, u32[]{:S(2)}, u32[]{:S(2)}) collective-permute-start(bf16[384,128]{1,0:T(8,128)(2,1)S(1)} %get-tuple-element.8), channel_id=1, source_target_pairs={{1,0},{3,2},{5,4},{7,6},{9,8},{11,10},{13,12},{15,14},{17,16},{19,... | collective-permute-start | bytes 294920 | tf_op jit(solution)/shard_map/ppermute | solution.py:13
  12.9 4.6 %collective-permute-start.1 = (bf16[384,128]{1,0:T(8,128)(2,1)S(1)}, bf16[384,128]{1,0:T(8,128)(2,1)S(1)}, u32[]{:S(2)}, u32[]{:S(2)}) collective-permute-start(bf16[384,128]{1,0:T(8,128)(2,1)S(1)} %get-tuple-element.9), channel_id=1, source_target_pairs={{0,1},{2,3},{4,5},{6,7},{8,9},{10,11},{12,13},{14,15},{16,17},{18,... | collective-permute-start | bytes 294920 | tf_op jit(solution)/shard_map/ppermute | solution.py:13
  17.4 1.5 %fusion.117 = (s32[1,1]{1,0:T(1,128)}, s32[1,1]{1,0:T(1,128)}, s32[1,1]{1,0:T(1,128)}, s32[1,1]{1,0:T(1,128)}, s32[1,1]{1,0:T(1,128)}, /*index=5*/s32[1,1]{1,0:T(1,128)}) fusion(s32[1,6]{1,0:T(1,128)} %param.9), kind=kLoop, calls=%fused_computation.94 | loop fusion | bytes 48 | tf_op jit(solution)/shard_map/slice | solution.py:68
  22.8 0.0 copy-done
  22.8 1.4 %fusion.6 = f32[7,128,128]{2,1,0:T(8,128)S(1)} fusion(bf16[1,2048,128]{2,1,0:T(8,128)(2,1)S(1)} %copy-done, bf16[1,2048,128]{2,1,0:T(8,128)(2,1)} %param.7), kind=kOutput, calls=%fused_computation.13 | convolution fusion | flops 67108864 | bytes 1114112 | tf_op jit(solution)/shard_map/dot_general | solution.py:22
  24.2 0.0 collective-permute-done
  24.2 1.3 %collective-permute-start.4 = (bf16[384,128]{1,0:T(8,128)(2,1)S(1)}, bf16[384,128]{1,0:T(8,128)(2,1)S(1)}, u32[]{:S(2)}, u32[]{:S(2)}) collective-permute-start(bf16[384,128]{1,0:T(8,128)(2,1)S(1)} %get-tuple-element.10), channel_id=1, source_target_pairs={{16,0},{18,2},{20,4},{22,6},{24,8},{26,10},{28,12},{30,14},{17,1},... | collective-permute-start | bytes 294920 | tf_op jit(solution)/shard_map/ppermute | solution.py:13
  25.5 0.0 copy-done.1
  25.5 1.5 %fusion.18 = f32[7,128,128]{2,1,0:T(8,128)S(1)} fusion(f32[7,128,128]{2,1,0:T(8,128)S(1)} %fusion.6, bf16[1,6,384,384]{3,2,1,0:T(8,128)(2,1)} %param.6, bf16[384,128]{1,0:T(8,128)(2,1)S(1)} %collective-permute-done, pred[384]{0:T(512)(128)(4,1)S(1)} %iota_compare_fusion.5, bf16[1,6,384,128]{3,2,1,0:T(8,128)(2,1)S(1)} %copy-done.1), kind=kOutput, calls=%fused_computation.25 | convolution fusion | flops 50479104 | bytes 558080 | tf_op jit(solution)/shard_map/dot_general | solution.py:22
  27.0 0.0 collective-permute-done.1
  27.0 1.4 %fusion.16 = f32[7,128,128]{2,1,0:T(8,128)S(1)} fusion(f32[7,128,128]{2,1,0:T(8,128)S(1)} %fusion.18, bf16[1,6,384,384]{3,2,1,0:T(8,128)(2,1)} %param.6, bf16[384,128]{1,0:T(8,128)(2,1)S(1)} %collective-permute-done.1, pred[384]{0:T(512)(128)(4,1)S(1)} %iota_compare_fusion.4, bf16[1,6,384,128]{3,2,1,0:T(8,128)(2,1)S(1)} %copy-done.1), kind=kOutput, calls=%fused_computation.23 | convolution fusion | flops 50479104 | bytes 558080 | tf_op jit(solution)/shard_map/dot_general | solution.py:22
  28.4 0.0 collective-permute-done.2
  28.4 1.5 %fusion.14 = f32[7,128,128]{2,1,0:T(8,128)S(1)} fusion(f32[7,128,128]{2,1,0:T(8,128)S(1)} %fusion.16, bf16[1,6,384,384]{3,2,1,0:T(8,128)(2,1)} %param.6, bf16[384,128]{1,0:T(8,128)(2,1)S(1)} %collective-permute-done.2, pred[384]{0:T(512)(128)(4,1)S(1)} %iota_compare_fusion.3, bf16[1,6,384,128]{3,2,1,0:T(8,128)(2,1)S(1)} %copy-done.1), kind=kOutput, calls=%fused_computation.21 | convolution fusion | flops 50479104 | bytes 558080 | tf_op jit(solution)/shard_map/dot_general | solution.py:22
  29.9 0.0 collective-permute-done.3
  29.9 1.4 %fusion.12 = f32[7,128,128]{2,1,0:T(8,128)S(1)} fusion(f32[7,128,128]{2,1,0:T(8,128)S(1)} %fusion.14, bf16[1,6,384,384]{3,2,1,0:T(8,128)(2,1)} %param.6, bf16[384,128]{1,0:T(8,128)(2,1)S(1)} %collective-permute-done.3, pred[384]{0:T(512)(128)(4,1)S(1)} %iota_compare_fusion.2, bf16[1,6,384,128]{3,2,1,0:T(8,128)(2,1)S(1)} %copy-done.1), kind=kOutput, calls=%fused_computation.19 | convolution fusion | flops 50479104 | bytes 558080 | tf_op jit(solution)/shard_map/dot_general | solution.py:22
  31.3 3.0 %collective-permute-done.4 = bf16[384,128]{1,0:T(8,128)(2,1)S(1)} collective-permute-done((bf16[384,128]{1,0:T(8,128)(2,1)S(1)}, bf16[384,128]{1,0:T(8,128)(2,1)S(1)}, u32[]{:S(2)}, u32[]{:S(2)}) %collective-permute-start.4) | collective-permute-done | bytes 98336 | tf_op jit(solution)/shard_map/ppermute | solution.py:13
  34.4 1.5 %fusion.10 = f32[7,128,128]{2,1,0:T(8,128)S(1)} fusion(f32[7,128,128]{2,1,0:T(8,128)S(1)} %fusion.12, bf16[1,6,384,384]{3,2,1,0:T(8,128)(2,1)} %param.6, bf16[384,128]{1,0:T(8,128)(2,1)S(1)} %collective-permute-done.4, pred[384]{0:T(512)(128)(4,1)S(1)} %iota_compare_fusion.1, bf16[1,6,384,128]{3,2,1,0:T(8,128)(2,1)S(1)} %copy-done.1), kind=kOutput, calls=%fused_computation.17 | convolution fusion | flops 50479104 | bytes 558080 | tf_op jit(solution)/shard_map/dot_general | solution.py:22
  35.8 0.0 collective-permute-done.5
  35.8 1.4 %fusion.8 = f32[7,128,128]{2,1,0:T(8,128)S(1)} fusion(f32[7,128,128]{2,1,0:T(8,128)S(1)} %fusion.10, bf16[1,6,384,384]{3,2,1,0:T(8,128)(2,1)} %param.6, bf16[384,128]{1,0:T(8,128)(2,1)S(1)} %collective-permute-done.5, pred[384]{0:T(512)(128)(4,1)S(1)} %iota_compare_fusion, bf16[1,6,384,128]{3,2,1,0:T(8,128)(2,1)S(1)} %copy-done.1), kind=kOutput, calls=%fused_computation.15 | convolution fusion | flops 50479104 | bytes 558080 | tf_op jit(solution)/shard_map/dot_general | solution.py:22
  37.3 0.5 copy.11
  37.8 9.9 %all_to_all.18 = f32[1,7,128,128]{3,0,1,2:T(1,128)S(1)} all-to-all(f32[1,7,128,128]{3,0,1,2:T(1,128)S(1)} %copy.11), channel_id=1, replica_groups=mesh['sub'=16,'grp'=2] {'grp'}, dimensions={2} | all-to-all | bytes 917504 | tf_op jit(solution)/shard_map/all_to_all | solution.py:78
  47.7 0.8 %copy.13 = f32[2,7,64,128]{3,2,1,0:T(8,128)} copy(f32[2,7,64,128]{3,2,0,1:T(8,128)S(1)} %bitcast.103) | data formatting | bytes 917504 | tf_op jit(solution)/shard_map/all_to_all | solution.py:78
  (7 shorter events, 0.1 us)
Async XLA Ops:
  0.0 22.8 %copy-start = (bf16[1,2048,128]{2,1,0:T(8,128)(2,1)S(1)}, bf16[1,2048,128]{2,1,0:T(8,128)(2,1)}, u32[]{:S(2)}) copy-start(bf16[1,2048,128]{2,1,0:T(8,128)(2,1)} %param.8) | copy-start | bytes 1572868
  0.0 25.5 %copy-start.1 = (bf16[1,6,384,128]{3,2,1,0:T(8,128)(2,1)S(1)}, bf16[1,6,384,128]{3,2,1,0:T(8,128)(2,1)}, u32[]{:S(2)}) copy-start(bf16[1,6,384,128]{3,2,1,0:T(8,128)(2,1)} %param.5) | copy-start | bytes 1769476
  1.3 34.6 %collective-permute-start.5 = (bf16[384,128]{1,0:T(8,128)(2,1)S(1)}, bf16[384,128]{1,0:T(8,128)(2,1)S(1)}, u32[]{:S(2)}, u32[]{:S(2)}) collective-permute-start(bf16[384,128]{1,0:T(8,128)(2,1)S(1)} %get-tuple-element.5), channel_id=1, source_target_pairs={{0,16},{2,18},{4,20},{6,22},{8,24},{10,26},{12,28},{14,30},{1,17},... | collective-permute-start | bytes 294920 | tf_op jit(solution)/shard_map/ppermute | solution.py:13
  7.2 21.2 %collective-permute-start.2 = (bf16[384,128]{1,0:T(8,128)(2,1)S(1)}, bf16[384,128]{1,0:T(8,128)(2,1)S(1)}, u32[]{:S(2)}, u32[]{:S(2)}) collective-permute-start(bf16[384,128]{1,0:T(8,128)(2,1)S(1)} %get-tuple-element.6), channel_id=1, source_target_pairs={{2,0},{4,2},{6,4},{8,6},{10,8},{12,10},{14,12},{16,14},{18,16},{20... | collective-permute-start | bytes 294920 | tf_op jit(solution)/shard_map/ppermute | solution.py:13
  8.5 21.4 %collective-permute-start.3 = (bf16[384,128]{1,0:T(8,128)(2,1)S(1)}, bf16[384,128]{1,0:T(8,128)(2,1)S(1)}, u32[]{:S(2)}, u32[]{:S(2)}) collective-permute-start(bf16[384,128]{1,0:T(8,128)(2,1)S(1)} %get-tuple-element.7), channel_id=1, source_target_pairs={{0,2},{2,4},{4,6},{6,8},{8,10},{10,12},{12,14},{14,16},{16,18},{18... | collective-permute-start | bytes 294920 | tf_op jit(solution)/shard_map/ppermute | solution.py:13
  11.6 12.6 %collective-permute-start = (bf16[384,128]{1,0:T(8,128)(2,1)S(1)}, bf16[384,128]{1,0:T(8,128)(2,1)S(1)}, u32[]{:S(2)}, u32[]{:S(2)}) collective-permute-start(bf16[384,128]{1,0:T(8,128)(2,1)S(1)} %get-tuple-element.8), channel_id=1, source_target_pairs={{1,0},{3,2},{5,4},{7,6},{9,8},{11,10},{13,12},{15,14},{17,16},{19,... | collective-permute-start | bytes 294920 | tf_op jit(solution)/shard_map/ppermute | solution.py:13
  12.9 14.1 %collective-permute-start.1 = (bf16[384,128]{1,0:T(8,128)(2,1)S(1)}, bf16[384,128]{1,0:T(8,128)(2,1)S(1)}, u32[]{:S(2)}, u32[]{:S(2)}) collective-permute-start(bf16[384,128]{1,0:T(8,128)(2,1)S(1)} %get-tuple-element.9), channel_id=1, source_target_pairs={{0,1},{2,3},{4,5},{6,7},{8,9},{10,11},{12,13},{14,15},{16,17},{18,... | collective-permute-start | bytes 294920 | tf_op jit(solution)/shard_map/ppermute | solution.py:13
  24.2 10.2 %collective-permute-start.4 = (bf16[384,128]{1,0:T(8,128)(2,1)S(1)}, bf16[384,128]{1,0:T(8,128)(2,1)S(1)}, u32[]{:S(2)}, u32[]{:S(2)}) collective-permute-start(bf16[384,128]{1,0:T(8,128)(2,1)S(1)} %get-tuple-element.10), channel_id=1, source_target_pairs={{16,0},{18,2},{20,4},{22,6},{24,8},{26,10},{28,12},{30,14},{17,1},... | collective-permute-start | bytes 294920 | tf_op jit(solution)/shard_map/ppermute | solution.py:13
where the time goes:
time: 49.1 us; the launch traced here: 48.5 us
  starting transfers between devices  17.4 us (35%)
  matrix products  10.1 us (21%)
  blocking collectives  9.92 us (20%)
  local copies, waits for them, and re-layouts  4.1 us (8%)
  between operations  3.94 us (8%)
  waiting for transfers between devices  3.03 us (6%)
    ppermute x6, starting transfers between devices, shifted(): lax.ppermute(value, axis, [(source, source + steps) for source in range(i...  17.4 us
    dot_general x7, matrix products, contract_rows(): lax.dot_general(left, right, (((0,), (0,)), ((), ())), preferred_element_...  10.1 us
    all_to_all x1, blocking collectives, local(): lax.all_to_all(coarse, 'grp', split_axis=2, concat_axis=0, tiled=True)  9.92 us
    ppermute x6, waiting for transfers between devices, shifted(): lax.ppermute(value, axis, [(source, source + steps) for source in range(i...  3.03 us
    slice x1, local copies, waits for them, and re-layouts, local(): counts[lower]  1.53 us
    squeeze x1, local copies, waits for them, and re-layouts, local(): own_margin[upper]  1.26 us
  transfers between devices with their start and end apart: 6, of which 1 were waited for; matrix products, arithmetic and copies ran while one was open for 21% of the time, Pallas kernels for 0%

commit v1 on v0

v1 whole, which is shorter than its diff:
```python
import functools

import jax
import jax.numpy as jnp
from jax import lax
from jax.experimental import pallas as pl
from jax.experimental.pallas import tpu as pltpu
from jax.sharding import PartitionSpec as P

ROW_TILE = 128
SPAN = 8
MESH = pl.DeviceIdType.MESH
F32 = jnp.float32
BF16 = jnp.bfloat16


def contract_rows(left, right):
    return lax.dot_general(left, right, (((0,), (0,)), ((), ())), preferred_element_type=F32)


def masked(block, tile_count):
    row_index = lax.broadcasted_iota(jnp.int32, block.shape, 0)
    return jnp.where(row_index < tile_count * ROW_TILE, block, jnp.zeros((), block.dtype))


def kernel(
    lines, group,
    counts, margin, matrix, own_basis, own_image, out,
    m_own, m_got, mats, basis, image, applied, stage,
    load_sem, margin_send, margin_recv, block_send, block_recv,
):
    q = lax.axis_index("sub")
    g = lax.axis_index("grp")
    odd = lax.rem(q, 2) == 1

    directions = (
        (odd, g >= 1, g + 1 < group, (0, 1)),
        (True, q >= 1, q + 1 < lines, (1, 0)),
        (odd, q >= SPAN, q + SPAN < lines, (SPAN, 0)),
    )

    def cases(j):
        up, low, high, _ = directions[j]
        if up is True:
            return ((True, low, high),)
        return (
            (True, jnp.logical_and(up, low), jnp.logical_and(up, high)),
            (False, jnp.logical_and(jnp.logical_not(up), high), jnp.logical_and(jnp.logical_not(up), low)),
        )

    def other(d):
        return lax.rem(g + d, group)

    barrier = pltpu.get_barrier_semaphore()
    for d in range(1, group):
        pl.semaphore_signal(barrier, inc=1, device_id=(q, other(d)), device_id_type=MESH)
    greeted = jnp.int32(group - 1)
    for j in (1, 2):
        _, low, high, (step, _) = directions[j]
        for there, line in ((low, q - step), (high, q + step)):
            @pl.when(there)
            def _():
                for d in range(group):
                    pl.semaphore_signal(barrier, inc=1, device_id=(line, other(d)), device_id_type=MESH)
            greeted = greeted + jnp.where(there, group, 0)

    load_basis = pltpu.make_async_copy(own_basis.at[0], basis, load_sem.at[6])
    load_image = pltpu.make_async_copy(own_image.at[0], image, load_sem.at[7])

    def loads(j, up):
        slot = 2 * j + (1 if up else 0)
        return (
            pltpu.make_async_copy(margin.at[0, slot], m_own.at[j], load_sem.at[2 * j]),
            pltpu.make_async_copy(matrix.at[0, slot], mats.at[j], load_sem.at[2 * j + 1]),
        )

    load_basis.start()
    load_image.start()
    for j in (1, 0, 2):
        for up, computes, _ in cases(j):
            @pl.when(computes)
            def _():
                for copy in loads(j, up):
                    copy.start()

    def margin_copy(j, up):
        sq, sg = directions[j][3]
        target = (q + sq, g + sg) if up else (q - sq, g - sg)
        slot = 2 * j + (0 if up else 1)
        return pltpu.make_async_remote_copy(
            src_ref=margin.at[0, slot], dst_ref=m_got.at[j],
            send_sem=margin_send.at[j], recv_sem=margin_recv.at[j],
            device_id=target, device_id_type=MESH,
        )

    pl.semaphore_wait(barrier, greeted)
    for j in (2, 1, 0):
        for up, _, sends in cases(j):
            @pl.when(sends)
            def _():
                margin_copy(j, up).start()

    def block_copies(block, line, own_line, place, slot):
        return [
            pltpu.make_async_remote_copy(
                src_ref=stage.at[block, other(d)], dst_ref=out.at[place, slot],
                send_sem=block_send.at[block, d], recv_sem=block_recv.at[place, slot],
                device_id=(line, other(d)), device_id_type=MESH,
            )
            for d in range(1 if own_line else 0, group)
        ]

    def deliver(block, value, line, own_line, place, slot):
        stage[block] = value.astype(BF16).reshape(stage.shape[1:])
        for copy in block_copies(block, line, own_line, place, slot):
            copy.start()
        if own_line:
            out[place, slot] = stage[block, g]

    def pair_targets(j, up):
        sq, sg = directions[j][3]
        lower = (q - sq, g - sg) if up else (q, g)
        upper = (q, g) if up else (q + sq, g + sg)
        own_lower = sq == 0 or not up
        own_upper = sq == 0 or up
        return (
            (1 + 2 * j, lower[0], own_lower, lower[1], 1 + 2 * j),
            (2 + 2 * j, upper[0], own_upper, upper[1], 2 + 2 * j),
        )

    load_basis.wait()
    load_image.wait()
    deliver(0, contract_rows(basis[...], image[...]), q, True, g, 0)

    nothing = jnp.zeros(out.shape[2:], BF16)
    out[group - 1, 1] = nothing
    out[0, 2] = nothing
    for j in (1, 2):
        _, low, high, _ = directions[j]
        for there, slot in ((high, 1 + 2 * j), (low, 2 + 2 * j)):
            @pl.when(jnp.logical_not(there))
            def _():
                for place in range(group):
                    out[place, slot] = nothing

    for j in (1, 0, 2):
        for up, computes, _ in cases(j):
            @pl.when(computes)
            def _():
                for copy in loads(j, up):
                    copy.wait()
                if up:
                    count = counts[0, 2 * j + 1]
                    product = contract_rows(mats[j], masked(m_own[j], count))
                    applied[j] = masked(product, count).astype(BF16)

    for j in (1, 0, 2):
        for up, computes, _ in cases(j):
            @pl.when(computes)
            def _():
                margin_copy(j, up).wait_recv()
                if up:
                    coupling = contract_rows(m_got[j], applied[j])
                else:
                    count = counts[0, 2 * j]
                    product = jnp.dot(mats[j], masked(m_got[j], count), preferred_element_type=F32)
                    coupling = contract_rows(m_own[j], masked(product, count).astype(BF16))
                first, second = pair_targets(j, up)
                deliver(first[0], coupling, *first[1:])
                deliver(second[0], coupling.T, *second[1:])

    def arrived(place, slot):
        pltpu.make_async_remote_copy(
            src_ref=stage.at[0, 0], dst_ref=out.at[place, slot],
            send_sem=block_send.at[0, 0], recv_sem=block_recv.at[place, slot],
            device_id=(q, other(1)), device_id_type=MESH,
        ).wait_recv()

    for d in range(1, group):
        arrived(other(d), 0)
    for place in range(group - 1):
        @pl.when(jnp.where(odd, place + 1, place) != g)
        def _():
            arrived(place, 1)
            arrived(place + 1, 2)
    for j in (1, 2):
        up, low, high, _ = directions[j]
        for at_upper in (True, False):
            if up is True:
                if not at_upper:
                    continue
                high_here, low_here = high, low
            else:
                chosen = up if at_upper else jnp.logical_not(up)
                high_here, low_here = jnp.logical_and(chosen, high), jnp.logical_and(chosen, low)

            @pl.when(high_here)
            def _():
                for d in range(0 if at_upper else 1, group):
                    arrived(other(d), 1 + 2 * j)

            @pl.when(low_here)
            def _():
                for d in range(1 if at_upper else 0, group):
                    arrived(other(d), 2 + 2 * j)

    for copy in block_copies(0, q, True, g, 0):
        copy.wait_send()
    for j in (1, 0, 2):
        for up, computes, sends in cases(j):
            @pl.when(sends)
            def _():
                margin_copy(j, up).wait_send()

            @pl.when(computes)
            def _():
                for target in pair_targets(j, up):
                    for copy in block_copies(*target):
                        copy.wait_send()


def local(lines, group, margin_basis, pair_matrix, own_basis, own_image, tile_counts):
    _, _, rows, eig = margin_basis.shape
    own_rows = own_basis.shape[1]
    share = eig // group
    blocks = pl.pallas_call(
        functools.partial(kernel, lines, group),
        out_shape=jax.ShapeDtypeStruct((group, 7, share, eig), BF16),
        in_specs=[pl.BlockSpec(memory_space=pltpu.SMEM)] + [pl.BlockSpec(memory_space=pltpu.HBM)] * 4,
        out_specs=pl.BlockSpec(memory_space=pltpu.VMEM),
        scratch_shapes=[
            pltpu.VMEM((3, rows, eig), BF16),
            pltpu.VMEM((3, rows, eig), BF16),
            pltpu.VMEM((3, rows, rows), BF16),
            pltpu.VMEM((own_rows, eig), BF16),
            pltpu.VMEM((own_rows, eig), BF16),
            pltpu.VMEM((3, rows, eig), BF16),
            pltpu.VMEM((7, group, share, eig), BF16),
            pltpu.SemaphoreType.DMA((8,)),
            pltpu.SemaphoreType.DMA((3,)),
            pltpu.SemaphoreType.DMA((3,)),
            pltpu.SemaphoreType.DMA((7, group)),
            pltpu.SemaphoreType.DMA((group, 7)),
        ],
        compiler_params=pltpu.CompilerParams(
            collective_id=0, has_side_effects=True, vmem_limit_bytes=24 * 1024 * 1024
        ),
    )(tile_counts, margin_basis, pair_matrix, own_basis, own_image)
    return blocks.astype(F32)


def solution(mesh):
    return jax.shard_map(
        functools.partial(local, mesh.shape["sub"], mesh.shape["grp"]),
        mesh=mesh,
        in_specs=(
            P(("sub", "grp"), None, None, None),
            P(("sub", "grp"), None, None, None),
            P(("sub", "grp"), None, None),
            P(("sub", "grp"), None, None),
            P(("sub", "grp"), None),
        ),
        out_specs=P("sub", None, "grp", None),
        check_vma=False,
    )
```

time: 49.1 us -> 19.6 us (0.40)
  the two profiles are of different devices: /device:TPU:0 before, /device:TPU:13 now
where the time goes in v1:
time: 19.6 us; the launch traced here: 19.3 us
  Pallas kernels  13.2 us (67%)
  local copies, waits for them, and re-layouts  5.28 us (27%)
  other arithmetic  0.81 us (4%)
    pallas_call x1, Pallas kernels, local(): pl.pallas_call(functools.partial(kernel, lines, group), out_shape=jax.Sha...  13.2 us
    unnamed x10, local copies, waits for them, and re-layouts  5.28 us
    convert_element_type x1, other arithmetic, local(): return blocks.astype(F32)  0.81 us

profile of v1, /device:TPU:13, one launch (start us, length us, event | category | flops | bytes accessed | tf_op | source)
XLA Modules:
  0.0 19.3 jit_solution(16915325164096375714)
XLA Ops:
  0.0 0.0 copy-start
  0.0 1.5 %copy-done = bf16[1,6,384,384]{3,2,1,0:T(8,128)(2,1)S(1)} copy-done((bf16[1,6,384,384]{3,2,1,0:T(8,128)(2,1)S(1)}, bf16[1,6,384,384]{3,2,1,0:T(8,128)(2,1)}, u32[]{:S(2)}) %copy-start) | copy-done | bytes 1769496
  1.5 0.0 copy-start.1
  1.5 1.1 %copy-done.1 = bf16[1,6,384,128]{3,2,1,0:T(8,128)(2,1)S(1)} copy-done((bf16[1,6,384,128]{3,2,1,0:T(8,128)(2,1)S(1)}, bf16[1,6,384,128]{3,2,1,0:T(8,128)(2,1)}, u32[]{:S(2)}) %copy-start.1) | copy-done | bytes 589848
  2.5 0.0 copy-start.2
  2.5 1.0 %copy-done.2 = bf16[1,2048,128]{2,1,0:T(8,128)(2,1)S(1)} copy-done((bf16[1,2048,128]{2,1,0:T(8,128)(2,1)S(1)}, bf16[1,2048,128]{2,1,0:T(8,128)(2,1)}, u32[]{:S(2)}) %copy-start.2) | copy-done | bytes 524312
  3.6 0.0 copy-start.3
  3.6 1.0 %copy-done.3 = bf16[1,2048,128]{2,1,0:T(8,128)(2,1)S(1)} copy-done((bf16[1,2048,128]{2,1,0:T(8,128)(2,1)S(1)}, bf16[1,2048,128]{2,1,0:T(8,128)(2,1)}, u32[]{:S(2)}) %copy-start.3) | copy-done | bytes 524312
  4.6 0.0 copy-start.4
  4.6 0.7 %copy-done.4 = s32[1,6]{1,0:T(1,128)S(1)} copy-done((s32[1,6]{1,0:T(1,128)S(1)}, s32[1,6]{1,0:T(1,128)}, u32[]{:S(2)}) %copy-start.4) | copy-done | bytes 48
  5.3 13.2 %shard_map.55 = bf16[2,7,64,128]{3,2,1,0:T(8,128)(2,1)S(1)} custom-call(s32[1,6]{1,0:T(1,128)S(1)} %copy-done.4, bf16[1,6,384,128]{3,2,1,0:T(8,128)(2,1)S(1)} %copy-done.1, bf16[1,6,384,384]{3,2,1,0:T(8,128)(2,1)S(1)} %copy-done, bf16[1,2048,128]{2,1,0:T(8,128)(2,1)S(1)} %copy-done.2, bf16[1,2048,128]{2,1,0:T(8,128)(2,1)S(1)} %copy-done.3), custom_call_target="tpu_custom_call" | custom-call | tf_op jit(solution)/shard_map/pallas_call | solution.py:226
  18.5 0.8 %convert_element_type.3 = f32[2,7,64,128]{3,2,1,0:T(8,128)} convert(bf16[2,7,64,128]{3,2,1,0:T(8,128)(2,1)S(1)} %shard_map.55) | non-fusion elementwise | flops 114688 | bytes 688128 | tf_op jit(solution)/shard_map/convert_element_type | solution.py:249
Async XLA Ops:
  0.0 1.5 %copy-start = (bf16[1,6,384,384]{3,2,1,0:T(8,128)(2,1)S(1)}, bf16[1,6,384,384]{3,2,1,0:T(8,128)(2,1)}, u32[]{:S(2)}) copy-start(bf16[1,6,384,384]{3,2,1,0:T(8,128)(2,1)} %matrix.1) | copy-start | bytes 5308420
  1.5 1.1 %copy-start.1 = (bf16[1,6,384,128]{3,2,1,0:T(8,128)(2,1)S(1)}, bf16[1,6,384,128]{3,2,1,0:T(8,128)(2,1)}, u32[]{:S(2)}) copy-start(bf16[1,6,384,128]{3,2,1,0:T(8,128)(2,1)} %margin.1) | copy-start | bytes 1769476
  2.5 1.0 %copy-start.2 = (bf16[1,2048,128]{2,1,0:T(8,128)(2,1)S(1)}, bf16[1,2048,128]{2,1,0:T(8,128)(2,1)}, u32[]{:S(2)}) copy-start(bf16[1,2048,128]{2,1,0:T(8,128)(2,1)} %own_basis.1) | copy-start | bytes 1572868
  3.6 1.0 %copy-start.3 = (bf16[1,2048,128]{2,1,0:T(8,128)(2,1)S(1)}, bf16[1,2048,128]{2,1,0:T(8,128)(2,1)}, u32[]{:S(2)}) copy-start(bf16[1,2048,128]{2,1,0:T(8,128)(2,1)} %own_image.1) | copy-start | bytes 1572868
  4.6 0.7 %copy-start.4 = (s32[1,6]{1,0:T(1,128)S(1)}, s32[1,6]{1,0:T(1,128)}, u32[]{:S(2)}) copy-start(s32[1,6]{1,0:T(1,128)} %counts.1) | copy-start | bytes 76

commit v2 on v1

--- a/solution.py
+++ b/solution.py
@@ -225,7 +225,7 @@
     share = eig // group
     blocks = pl.pallas_call(
         functools.partial(kernel, lines, group),
-        out_shape=jax.ShapeDtypeStruct((group, 7, share, eig), BF16),
+        out_shape=pltpu.VMEM((group, 7, share, eig), BF16),
         in_specs=[pl.BlockSpec(memory_space=pltpu.SMEM)] + [pl.BlockSpec(memory_space=pltpu.HBM)] * 4,
         out_specs=pl.BlockSpec(memory_space=pltpu.VMEM),
         scratch_shapes=[
@@ -243,7 +243,7 @@
             pltpu.SemaphoreType.DMA((group, 7)),
         ],
         compiler_params=pltpu.CompilerParams(
-            collective_id=0, has_side_effects=True, vmem_limit_bytes=24 * 1024 * 1024
+            collective_id=0, has_side_effects=True
         ),
     )(tile_counts, margin_basis, pair_matrix, own_basis, own_image)
     return blocks.astype(F32)

time: 19.6 us -> 14.5 us (0.74)
  local copies, waits for them, and re-layouts: 5.28 us -> 0 us
  Pallas kernels: 13.2 us -> 13.5 us
    unnamed x10 -> x0, local copies, waits for them, and re-layouts: 5.28 us -> none
    pallas_call x1, Pallas kernels: 13.2 us -> 13.5 us  [local(): pl.pallas_call(functools.partial(kernel, lines, group), out_shape=pltpu.V...]
where the time goes in v2:
time: 14.5 us; the launch traced here: 14.3 us
  Pallas kernels  13.5 us (93%)
  other arithmetic  0.81 us (6%)
    pallas_call x1, Pallas kernels, local(): pl.pallas_call(functools.partial(kernel, lines, group), out_shape=pltpu.V...  13.5 us
    convert_element_type x1, other arithmetic, local(): return blocks.astype(F32)  0.81 us

profile of v2, /device:TPU:13, one launch (start us, length us, event | category | flops | bytes accessed | tf_op | source)
XLA Modules:
  0.0 14.3 jit_solution(7460727900781288347)
XLA Ops:
  0.0 13.5 %shard_map.55 = bf16[2,7,64,128]{3,2,1,0:T(8,128)(2,1)S(1)} custom-call(s32[1,6]{1,0:T(1,128)} %counts.1, bf16[1,6,384,128]{3,2,1,0:T(8,128)(2,1)} %margin.1, bf16[1,6,384,384]{3,2,1,0:T(8,128)(2,1)} %matrix.1, bf16[1,2048,128]{2,1,0:T(8,128)(2,1)} %own_basis.1, bf16[1,2048,128]{2,1,0:T(8,128)(2,1)} %own_image.1), custom_call_target="tpu_custom_call" | custom-call | tf_op jit(solution)/shard_map/pallas_call | solution.py:226
  13.5 0.8 %convert_element_type.3 = f32[2,7,64,128]{3,2,1,0:T(8,128)} convert(bf16[2,7,64,128]{3,2,1,0:T(8,128)(2,1)S(1)} %shard_map.55) | non-fusion elementwise | flops 114688 | bytes 688128 | tf_op jit(solution)/shard_map/convert_element_type | solution.py:249

commit v3 on v2

--- a/solution.py
+++ b/solution.py
@@ -52,17 +52,17 @@
         return lax.rem(g + d, group)
 
     barrier = pltpu.get_barrier_semaphore()
+    greeted = jnp.int32(group - 1)
+    for j in (2, 1):
+        step = directions[j][3][0]
+        for up, computes, sends in cases(j):
+            @pl.when(computes)
+            def _():
+                source = (q - step, g) if up else (q + step, g)
+                pl.semaphore_signal(barrier, inc=1, device_id=source, device_id_type=MESH)
+            greeted = greeted + jnp.where(sends, 1, 0)
     for d in range(1, group):
         pl.semaphore_signal(barrier, inc=1, device_id=(q, other(d)), device_id_type=MESH)
-    greeted = jnp.int32(group - 1)
-    for j in (1, 2):
-        _, low, high, (step, _) = directions[j]
-        for there, line in ((low, q - step), (high, q + step)):
-            @pl.when(there)
-            def _():
-                for d in range(group):
-                    pl.semaphore_signal(barrier, inc=1, device_id=(line, other(d)), device_id_type=MESH)
-            greeted = greeted + jnp.where(there, group, 0)
 
     load_basis = pltpu.make_async_copy(own_basis.at[0], basis, load_sem.at[6])
     load_image = pltpu.make_async_copy(own_image.at[0], image, load_sem.at[7])
@@ -94,7 +94,7 @@
         )
 
     pl.semaphore_wait(barrier, greeted)
-    for j in (2, 1, 0):
+    for j in (1, 2, 0):
         for up, _, sends in cases(j):
             @pl.when(sends)
             def _():
@@ -107,7 +107,7 @@
                 send_sem=block_send.at[block, d], recv_sem=block_recv.at[place, slot],
                 device_id=(line, other(d)), device_id_type=MESH,
             )
-            for d in range(1 if own_line else 0, group)
+            for d in reversed(range(1 if own_line else 0, group))
         ]
 
     def deliver(block, value, line, own_line, place, slot):
@@ -166,8 +166,12 @@
                     product = jnp.dot(mats[j], masked(m_got[j], count), preferred_element_type=F32)
                     coupling = contract_rows(m_own[j], masked(product, count).astype(BF16))
                 first, second = pair_targets(j, up)
-                deliver(first[0], coupling, *first[1:])
-                deliver(second[0], coupling.T, *second[1:])
+                if up:
+                    deliver(first[0], coupling, *first[1:])
+                    deliver(second[0], coupling.T, *second[1:])
+                else:
+                    deliver(second[0], coupling.T, *second[1:])
+                    deliver(first[0], coupling, *first[1:])
 
     def arrived(place, slot):
         pltpu.make_async_remote_copy(

time: 14.5 us -> 13.3 us (0.917)
  Pallas kernels: 13.5 us -> 12.3 us
    pallas_call x1, Pallas kernels: 13.5 us -> 12.3 us  [local(): pl.pallas_call(functools.partial(kernel, lines, group), out_shape=pltpu.V...]
where the time goes in v3:
time: 13.3 us; the launch traced here: 13.1 us
  Pallas kernels  12.3 us (92%)
  other arithmetic  0.81 us (6%)
    pallas_call x1, Pallas kernels, local(): pl.pallas_call(functools.partial(kernel, lines, group), out_shape=pltpu.V...  12.3 us
    convert_element_type x1, other arithmetic, local(): return blocks.astype(F32)  0.81 us

profile of v3, /device:TPU:13, one launch (start us, length us, event | category | flops | bytes accessed | tf_op | source)
XLA Modules:
  0.0 13.1 jit_solution(71402536641225057)
XLA Ops:
  0.0 12.3 %shard_map.55 = bf16[2,7,64,128]{3,2,1,0:T(8,128)(2,1)S(1)} custom-call(s32[1,6]{1,0:T(1,128)} %counts.1, bf16[1,6,384,128]{3,2,1,0:T(8,128)(2,1)} %margin.1, bf16[1,6,384,384]{3,2,1,0:T(8,128)(2,1)} %matrix.1, bf16[1,2048,128]{2,1,0:T(8,128)(2,1)} %own_basis.1, bf16[1,2048,128]{2,1,0:T(8,128)(2,1)} %own_image.1), custom_call_target="tpu_custom_call" | custom-call | tf_op jit(solution)/shard_map/pallas_call | solution.py:230
  12.3 0.8 %convert_element_type.3 = f32[2,7,64,128]{3,2,1,0:T(8,128)} convert(bf16[2,7,64,128]{3,2,1,0:T(8,128)(2,1)S(1)} %shard_map.55) | non-fusion elementwise | flops 114688 | bytes 688128 | tf_op jit(solution)/shard_map/convert_element_type | solution.py:253

commit v4 on v3

--- a/solution.py
+++ b/solution.py
@@ -26,7 +26,7 @@
 def kernel(
     lines, group,
     counts, margin, matrix, own_basis, own_image, out,
-    m_own, m_got, mats, basis, image, applied, stage,
+    m_own, m_sent, m_got, mats, basis, image, applied, rest, stage,
     load_sem, margin_send, margin_recv, block_send, block_recv,
 ):
     q = lax.axis_index("sub")
@@ -67,6 +67,9 @@
     load_basis = pltpu.make_async_copy(own_basis.at[0], basis, load_sem.at[6])
     load_image = pltpu.make_async_copy(own_image.at[0], image, load_sem.at[7])
 
+    def sent_load(j, up):
+        return pltpu.make_async_copy(margin.at[0, 2 * j + (0 if up else 1)], m_sent.at[j], load_sem.at[8 + j])
+
     def loads(j, up):
         slot = 2 * j + (1 if up else 0)
         return (
@@ -74,6 +77,11 @@
             pltpu.make_async_copy(matrix.at[0, slot], mats.at[j], load_sem.at[2 * j + 1]),
         )
 
+    for j in (1, 2, 0):
+        for up, _, sends in cases(j):
+            @pl.when(sends)
+            def _():
+                sent_load(j, up).start()
     load_basis.start()
     load_image.start()
     for j in (1, 0, 2):
@@ -88,7 +96,7 @@
         target = (q + sq, g + sg) if up else (q - sq, g - sg)
         slot = 2 * j + (0 if up else 1)
         return pltpu.make_async_remote_copy(
-            src_ref=margin.at[0, slot], dst_ref=m_got.at[j],
+            src_ref=m_sent.at[j], dst_ref=m_got.at[j],
             send_sem=margin_send.at[j], recv_sem=margin_recv.at[j],
             device_id=target, device_id_type=MESH,
         )
@@ -98,6 +106,7 @@
         for up, _, sends in cases(j):
             @pl.when(sends)
             def _():
+                sent_load(j, up).wait()
                 margin_copy(j, up).start()
 
     def block_copies(block, line, own_line, place, slot):
@@ -153,6 +162,11 @@
                     count = counts[0, 2 * j + 1]
                     product = contract_rows(mats[j], masked(m_own[j], count))
                     applied[j] = masked(product, count).astype(BF16)
+                else:
+                    count = counts[0, 2 * j]
+                    product = masked(contract_rows(mats[j], masked(m_own[j], count)), count)
+                    applied[j] = product.astype(BF16)
+                    rest[j] = (product - applied[j].astype(F32)).astype(BF16)
 
     for j in (1, 0, 2):
         for up, computes, _ in cases(j):
@@ -162,9 +176,7 @@
                 if up:
                     coupling = contract_rows(m_got[j], applied[j])
                 else:
-                    count = counts[0, 2 * j]
-                    product = jnp.dot(mats[j], masked(m_got[j], count), preferred_element_type=F32)
-                    coupling = contract_rows(m_own[j], masked(product, count).astype(BF16))
+                    coupling = contract_rows(applied[j], m_got[j]) + contract_rows(rest[j], m_got[j])
                 first, second = pair_targets(j, up)
                 if up:
                     deliver(first[0], coupling, *first[1:])
@@ -235,12 +247,14 @@
         scratch_shapes=[
             pltpu.VMEM((3, rows, eig), BF16),
             pltpu.VMEM((3, rows, eig), BF16),
+            pltpu.VMEM((3, rows, eig), BF16),
             pltpu.VMEM((3, rows, rows), BF16),
             pltpu.VMEM((own_rows, eig), BF16),
             pltpu.VMEM((own_rows, eig), BF16),
             pltpu.VMEM((3, rows, eig), BF16),
+            pltpu.VMEM((3, rows, eig), BF16),
             pltpu.VMEM((7, group, share, eig), BF16),
-            pltpu.SemaphoreType.DMA((8,)),
+            pltpu.SemaphoreType.DMA((11,)),
             pltpu.SemaphoreType.DMA((3,)),
             pltpu.SemaphoreType.DMA((3,)),
             pltpu.SemaphoreType.DMA((7, group)),

time: 13.3 us -> 13.2 us (level)
  Pallas kernels: 12.3 us -> 12.1 us
    pallas_call x1, Pallas kernels: 12.3 us -> 12.1 us  [local(): pl.pallas_call(functools.partial(kernel, lines, group), out_shape=pltpu.V...]
where the time goes in v4:
time: 13.2 us; the launch traced here: 13 us
  Pallas kernels  12.1 us (92%)
  other arithmetic  0.81 us (6%)
    pallas_call x1, Pallas kernels, local(): pl.pallas_call(functools.partial(kernel, lines, group), out_shape=pltpu.V...  12.1 us
    convert_element_type x1, other arithmetic, local(): return blocks.astype(F32)  0.81 us

profile of v4, /device:TPU:13, one launch (start us, length us, event | category | flops | bytes accessed | tf_op | source)
XLA Modules:
  0.0 13.0 jit_solution(9187640432008856755)
XLA Ops:
  0.0 12.1 %shard_map.55 = bf16[2,7,64,128]{3,2,1,0:T(8,128)(2,1)S(1)} custom-call(s32[1,6]{1,0:T(1,128)} %counts.1, bf16[1,6,384,128]{3,2,1,0:T(8,128)(2,1)} %margin.1, bf16[1,6,384,384]{3,2,1,0:T(8,128)(2,1)} %matrix.1, bf16[1,2048,128]{2,1,0:T(8,128)(2,1)} %own_basis.1, bf16[1,2048,128]{2,1,0:T(8,128)(2,1)} %own_image.1), custom_call_target="tpu_custom_call" | custom-call | tf_op jit(solution)/shard_map/pallas_call | solution.py:242
  12.1 0.8 %convert_element_type.3 = f32[2,7,64,128]{3,2,1,0:T(8,128)} convert(bf16[2,7,64,128]{3,2,1,0:T(8,128)(2,1)S(1)} %shard_map.55) | non-fusion elementwise | flops 114688 | bytes 688128 | tf_op jit(solution)/shard_map/convert_element_type | solution.py:267
